TPU v7x, 32 devices: a whole 2x2x4 slice. The times are simulated.
32 devices in a mesh: blk: 32 (over z, y, x, core).
Axes of the slice: x: 2, y: 2, z: 4, core: 2. Of those that a mesh axis runs over, the one named last changes fastest.
Arguments:
- features: float32 [8192, 128], P('blk'), may hold values from -6 to 6
- weight_one: float32 [128, 128], replicated, may hold values from -0.5 to 0.5
- weight_two: float32 [128, 128], replicated, may hold values from -0.5 to 0.5
- dense_tiles: bfloat16 [1024, 128, 128], P('blk'), may hold values from -0.078125 to 0.078125
- dense_row: int32 [1024], P('blk'), may hold values from 0 to 1
- hub_block: int32 [32], replicated, may hold values from 0 to 1
- sparse_tiles: bfloat16 [3584, 128, 128], P('blk'), may hold values from -0.078125 to 0.078125
- sparse_row: int32 [3584], P('blk'), may hold values from 0 to 1
- sparse_src: int32 [3584], P('blk'), may hold values from 0 to 5
- sparse_count: int32 [32], P('blk'), may hold values from 1 to 112, as said below
- fetch_list: int32 [32, 4], P('blk'), may hold values from 0 to 1
Outputs:
- embedded: float32 [8192, 128], P('blk')
Inputs may be any that keep to these rules, and one draw needn't show every extreme that they name: `sparse_count`: one device has exactly 112 live slots.
All inputs are finite; a program needn't handle non-finite values.
Results may differ from a plain program's by a relative error of at most 0.0041.
Values may be sent and summed in bfloat16 or wider, within the bound.
A program may use at most 128 MiB of HBM per device.

v0:
```python
import jax
import jax.numpy as jnp
from jax import lax
from jax.sharding import PartitionSpec as P

F = 128
TILE = 128
NB = 2
KS = 112
HOPS = 2
FETCH = 1


def from_behind(shard, axis, by):
    size = lax.axis_size(axis)
    return lax.ppermute(shard, axis, [(i, (i + by) % size) for i in range(size)])


def neighbour_offsets():
    return list(range(-HOPS, 0)) + list(range(1, HOPS + 1))


def accumulate(running, tile_set, row_ids, inputs, slot_mask):
    products = jnp.einsum("sij,sjf->sif", tile_set, inputs, preferred_element_type=jnp.float32)
    block_ids = jnp.arange(running.shape[0], dtype=jnp.int32)
    onehot = (row_ids[:, None] == block_ids[None, :]).astype(jnp.float32) * slot_mask[:, None]
    return running + jnp.einsum("sn,sif->nif", onehot, products, precision=lax.Precision.HIGHEST)


def shards(
    features,
    weight_one,
    weight_two,
    dense_tiles,
    dense_row,
    hub_block,
    sparse_tiles,
    sparse_row,
    sparse_src,
    sparse_count,
    fetch_list,
):
    own_index = lax.axis_index("blk")
    offsets = neighbour_offsets()
    wanted_lists = [fetch_list[0, entry * FETCH : (entry + 1) * FETCH] for entry in range(2 * HOPS)]

    def propagate(hidden_rows, weight):
        blocks = hidden_rows.reshape(NB, TILE, F)
        zero_sums = jnp.zeros((NB, TILE, F), jnp.float32)
        hub_here = lax.dynamic_index_in_dim(hub_block, own_index, 0, keepdims=False)
        hub_rows = lax.dynamic_index_in_dim(blocks, hub_here, 0, keepdims=False)
        stripe = lax.all_gather(hub_rows, "blk", axis=0, tiled=True)
        shard_total = stripe.shape[0] // TILE
        summed = accumulate(
            zero_sums,
            dense_tiles,
            dense_row,
            stripe.reshape(shard_total, TILE, F),
            jnp.ones((shard_total,), jnp.float32),
        )
        fetched = [
            from_behind(blocks, "blk", -offsets[entry])[wanted_lists[entry]]
            for entry in range(2 * HOPS)
        ]
        gathered_blocks = jnp.concatenate([blocks] + fetched, axis=0)
        live_total = sparse_count[0]
        live_mask = (jnp.arange(KS, dtype=jnp.int32) < live_total).astype(jnp.float32)
        summed = accumulate(
            summed, sparse_tiles, sparse_row, gathered_blocks[sparse_src], live_mask
        )
        projected = jnp.dot(
            summed.reshape(NB * TILE, F),
            weight,
            precision=lax.Precision.HIGHEST,
            preferred_element_type=jnp.float32,
        )
        return jax.nn.relu(projected)

    hidden = propagate(features.astype(jnp.bfloat16), weight_one).astype(jnp.bfloat16)
    return propagate(hidden, weight_two)


def solution(mesh):
    placed = (
        P("blk", None),
        P(),
        P(),
        P("blk", None, None),
        P("blk"),
        P(),
        P("blk", None, None),
        P("blk"),
        P("blk"),
        P("blk"),
        P("blk", None),
    )
    return jax.shard_map(
        shards, mesh=mesh, in_specs=placed, out_specs=P("blk", None), check_vma=False
    )
```

profile of v0, /device:TPU:0, one launch (start us, length us, event | category | flops | bytes accessed | tf_op | source)
XLA Modules:
  0.0 147.7 jit_solution(14858714495938051999)
XLA Ops:
  6.5 0.0 copy-start
  6.5 0.0 all-gather.5.cloned.1.call-start
  6.5 1.0 convert_element_type.18
  7.5 2.9 %collective-permute-start = (bf16[2,128,128]{2,1,0:T(8,128)(2,1)S(1)}, bf16[2,128,128]{2,1,0:T(8,128)(2,1)S(1)}, u32[]{:S(2)}, u32[]{:S(2)}) collective-permute-start(bf16[2,128,128]{2,1,0:T(8,128)(2,1)S(1)} %bitcast.58), channel_id=1, source_target_pairs={{0,2},{1,3},{2,4},{3,5},{4,6},{5,7},{6,8},{7,9},{8,10},{9,11},{10,... | collective-permute-start | bytes 196616 | tf_op jit(solution)/shard_map/ppermute | solution.py:16
  10.5 0.0 collective-permute-start.1
  10.5 5.3 %collective-permute-start.2 = (bf16[2,128,128]{2,1,0:T(8,128)(2,1)S(1)}, bf16[2,128,128]{2,1,0:T(8,128)(2,1)S(1)}, u32[]{:S(2)}, u32[]{:S(2)}) collective-permute-start(bf16[2,128,128]{2,1,0:T(8,128)(2,1)S(1)} %bitcast.60), channel_id=1, source_target_pairs={{0,31},{1,0},{2,1},{3,2},{4,3},{5,4},{6,5},{7,6},{8,7},{9,8},{10,9... | collective-permute-start | bytes 196616 | tf_op jit(solution)/shard_map/ppermute | solution.py:16
  15.8 0.5 collective-permute-start.3
  16.3 1.2 dynamic_slice.12
  19.5 0.6 constant_dynamic-slice_fusion.1
  20.1 0.0 all-gather.5.cloned.1.call-update
  20.1 0.0 all-gather.7.cloned.1.call-start
  20.2 1.5 %fusion.30 = (s32[1,1]{1,0:T(1,128)}, s32[1,1]{1,0:T(1,128)}, s32[1,1]{1,0:T(1,128)}, s32[1,1]{1,0:T(1,128)}) fusion(s32[1,4]{1,0:T(1,128)} %param.21), kind=kLoop, calls=%fused_computation.45 | loop fusion | bytes 32 | tf_op jit(solution)/shard_map/slice | solution.py:45
  30.0 0.7 compare_select_fusion
  30.7 0.0 collective-permute-done
  30.7 0.0 collective-permute-done.1
  30.7 0.0 collective-permute-done.2
  30.8 0.0 collective-permute-done.3
  30.8 3.0 %gather_fusion = bf16[112,128,128]{2,1,0:T(8,128)(2,1)} fusion(bf16[6,128,128]{2,1,0:T(8,128)(2,1)S(1)} %dynamic-slice_dynamic-update-slice_fusion.4, s32[1024]{0:T(1024)S(1)} %pad_clamp_fusion), kind=kCustom, calls=%fused_computation | custom fusion | bytes 7340480 | tf_op jit(solution)/shard_map/gather | solution.py:69
  33.8 8.8 %fusion.32 = f32[112,128,128]{2,1,0:T(8,128)} fusion(bf16[112,128,128]{2,1,0:T(8,128)(2,1)} %gather_fusion, bf16[112,128,128]{2,1,0:T(8,128)(2,1)} %param.17), kind=kOutput, calls=%fused_computation.47 | convolution fusion | flops 469762048 | bytes 14680064 | tf_op jit(solution)/shard_map/sij,sjf->sif/dot_general | solution.py:24
  42.6 8.5 %copy.15 = f32[112,128,128]{1,0,2:T(8,128)} copy(f32[112,128,128]{2,1,0:T(8,128)} %fusion.32) | data formatting | bytes 14680064 | tf_op jit(solution)/shard_map/sij,sjf->sif/dot_general | solution.py:24
  51.1 0.0 copy-done.3
  51.1 5.7 %fusion.2 = f32[2,128,128]{2,0,1:T(2,128)S(1)} fusion(f32[112,128,128]{1,0,2:T(8,128)} %copy.15, f32[112]{0:T(128)S(1)} %compare_convert_fusion, s32[112]{0:T(128)S(1)} %copy-done.3), kind=kOutput, calls=%fused_computation.4 | convolution fusion | flops 44040640 | bytes 7472000 | tf_op jit(solution)/shard_map/sn,sif->nif/dot_general | solution.py:27
  56.8 15.7 %all-gather.5.cloned.1.call-done = bf16[1,4096,128]{2,1,0:T(8,128)(2,1)} async-done(((bf16[1,128,128]{2,1,0:T(8,128)(2,1)}), bf16[1,4096,128]{2,1,0:T(8,128)(2,1)}) %all-gather.5.cloned.1.call-update) | async-done | bytes 1048592 | tf_op jit(solution)/shard_map/all_gather | solution.py:52
  72.6 0.0 copy-done
  72.6 3.5 %fusion.31 = f32[32,128,128]{2,1,0:T(8,128)} fusion(bf16[32,128,128]{2,1,0:T(8,128)(2,1)} %bitcast.54, bf16[32,128,128]{2,1,0:T(8,128)(2,1)S(1)} %copy-done), kind=kOutput, calls=%fused_computation.46 | convolution fusion | flops 134217728 | bytes 4194304 | tf_op jit(solution)/shard_map/sij,sjf->sif/dot_general | solution.py:24
  76.0 2.4 %copy.14 = f32[32,128,128]{1,0,2:T(8,128)S(1)} copy(f32[32,128,128]{2,1,0:T(8,128)} %fusion.31) | data formatting | bytes 4194304 | tf_op jit(solution)/shard_map/sij,sjf->sif/dot_general | solution.py:24
  78.4 0.0 copy-done.4
  78.4 0.8 fusion.8
  79.3 0.3 fusion.14
  79.6 0.6 constant_dynamic-slice_fusion
  80.2 0.0 all-gather.7.cloned.1.call-update
  80.2 1.3 collective-permute-start.4
  81.5 0.0 collective-permute-start.5
  81.5 5.3 %collective-permute-start.6 = (bf16[2,128,128]{2,1,0:T(8,128)(2,1)S(1)}, bf16[2,128,128]{2,1,0:T(8,128)(2,1)S(1)}, u32[]{:S(2)}, u32[]{:S(2)}) collective-permute-start(bf16[2,128,128]{2,1,0:T(8,128)(2,1)S(1)} %bitcast.67), channel_id=1, source_target_pairs={{0,31},{1,0},{2,1},{3,2},{4,3},{5,4},{6,5},{7,6},{8,7},{9,8},{10,9... | collective-permute-start | bytes 196616 | tf_op jit(solution)/shard_map/ppermute | solution.py:16
  86.9 0.7 collective-permute-start.7
  87.6 0.6 collective-permute-done.4
  88.2 0.7 collective-permute-done.5
  89.0 0.1 collective-permute-done.6
  89.0 2.3 %collective-permute-done.7 = bf16[2,128,128]{2,1,0:T(8,128)(2,1)S(1)} collective-permute-done((bf16[2,128,128]{2,1,0:T(8,128)(2,1)S(1)}, bf16[2,128,128]{2,1,0:T(8,128)(2,1)S(1)}, u32[]{:S(2)}, u32[]{:S(2)}) %collective-permute-start.7) | collective-permute-done | bytes 65568 | tf_op jit(solution)/shard_map/ppermute | solution.py:16
  91.4 3.0 %gather_fusion.1 = bf16[112,128,128]{2,1,0:T(8,128)(2,1)} fusion(bf16[6,128,128]{2,1,0:T(8,128)(2,1)S(1)} %dynamic-slice_dynamic-update-slice_fusion, s32[1024]{0:T(1024)S(1)} %pad_clamp_fusion), kind=kCustom, calls=%fused_computation.1 | custom fusion | bytes 7340480 | tf_op jit(solution)/shard_map/gather | solution.py:69
  94.3 8.8 %fusion.34 = f32[112,128,128]{2,1,0:T(8,128)} fusion(bf16[112,128,128]{2,1,0:T(8,128)(2,1)} %gather_fusion.1, bf16[112,128,128]{2,1,0:T(8,128)(2,1)} %param.17), kind=kOutput, calls=%fused_computation.49 | convolution fusion | flops 469762048 | bytes 14680064 | tf_op jit(solution)/shard_map/sij,sjf->sif/dot_general | solution.py:24
  103.1 8.5 %copy.17 = f32[112,128,128]{1,0,2:T(8,128)} copy(f32[112,128,128]{2,1,0:T(8,128)} %fusion.34) | data formatting | bytes 14680064 | tf_op jit(solution)/shard_map/sij,sjf->sif/dot_general | solution.py:24
  111.7 5.7 %fusion = f32[2,128,128]{2,0,1:T(2,128)S(1)} fusion(f32[112,128,128]{1,0,2:T(8,128)} %copy.17, f32[112]{0:T(128)S(1)} %compare_convert_fusion, s32[112]{0:T(128)S(1)} %copy-done.3), kind=kOutput, calls=%fused_computation.2 | convolution fusion | flops 44040640 | bytes 7472000 | tf_op jit(solution)/shard_map/sn,sif->nif/dot_general | solution.py:27
  117.4 15.9 %all-gather.7.cloned.1.call-done = bf16[1,4096,128]{2,1,0:T(8,128)(2,1)} async-done(((bf16[1,128,128]{2,1,0:T(8,128)(2,1)}), bf16[1,4096,128]{2,1,0:T(8,128)(2,1)}) %all-gather.7.cloned.1.call-update) | async-done | bytes 1048592 | tf_op jit(solution)/shard_map/all_gather | solution.py:52
  133.2 3.4 %fusion.33 = f32[32,128,128]{2,1,0:T(8,128)} fusion(bf16[32,128,128]{2,1,0:T(8,128)(2,1)} %bitcast.55, bf16[32,128,128]{2,1,0:T(8,128)(2,1)S(1)} %copy-done), kind=kOutput, calls=%fused_computation.48 | convolution fusion | flops 134217728 | bytes 4194304 | tf_op jit(solution)/shard_map/sij,sjf->sif/dot_general | solution.py:24
  136.7 2.4 %copy.16 = f32[32,128,128]{1,0,2:T(8,128)S(1)} copy(f32[32,128,128]{2,1,0:T(8,128)} %fusion.33) | data formatting | bytes 4194304 | tf_op jit(solution)/shard_map/sij,sjf->sif/dot_general | solution.py:24
  139.1 0.8 fusion.11
  139.9 0.9 convolution_maximum_fusion
  (20 shorter events, 0.2 us)
Async XLA Ops:
  6.5 66.0 %copy-start = (bf16[32,128,128]{2,1,0:T(8,128)(2,1)S(1)}, bf16[32,128,128]{2,1,0:T(8,128)(2,1)}, u32[]{:S(2)}) copy-start(bf16[32,128,128]{2,1,0:T(8,128)(2,1)} %param.14) | copy-start | bytes 3145732
  6.5 66.0 %all-gather.5.cloned.1.call-start = ((), (), s32[]{:S(2)}) async-start(), calls=%async_computation | async-start | bytes 1081344 | tf_op jit(solution)/shard_map/all_gather | solution.py:52
  7.5 23.1 %collective-permute-start = (bf16[2,128,128]{2,1,0:T(8,128)(2,1)S(1)}, bf16[2,128,128]{2,1,0:T(8,128)(2,1)S(1)}, u32[]{:S(2)}, u32[]{:S(2)}) collective-permute-start(bf16[2,128,128]{2,1,0:T(8,128)(2,1)S(1)} %bitcast.58), channel_id=1, source_target_pairs={{0,2},{1,3},{2,4},{3,5},{4,6},{5,7},{6,8},{7,9},{8,10},{9,11},{10,... | collective-permute-start | bytes 196616 | tf_op jit(solution)/shard_map/ppermute | solution.py:16
  10.5 20.2 %collective-permute-start.1 = (bf16[2,128,128]{2,1,0:T(8,128)(2,1)S(1)}, bf16[2,128,128]{2,1,0:T(8,128)(2,1)S(1)}, u32[]{:S(2)}, u32[]{:S(2)}) collective-permute-start(bf16[2,128,128]{2,1,0:T(8,128)(2,1)S(1)} %bitcast.59), channel_id=1, source_target_pairs={{0,1},{1,2},{2,3},{3,4},{4,5},{5,6},{6,7},{7,8},{8,9},{9,10},{10,1... | collective-permute-start | bytes 196616 | tf_op jit(solution)/shard_map/ppermute | solution.py:16
  10.5 20.3 %collective-permute-start.2 = (bf16[2,128,128]{2,1,0:T(8,128)(2,1)S(1)}, bf16[2,128,128]{2,1,0:T(8,128)(2,1)S(1)}, u32[]{:S(2)}, u32[]{:S(2)}) collective-permute-start(bf16[2,128,128]{2,1,0:T(8,128)(2,1)S(1)} %bitcast.60), channel_id=1, source_target_pairs={{0,31},{1,0},{2,1},{3,2},{4,3},{5,4},{6,5},{7,6},{8,7},{9,8},{10,9... | collective-permute-start | bytes 196616 | tf_op jit(solution)/shard_map/ppermute | solution.py:16
  15.8 15.0 %collective-permute-start.3 = (bf16[2,128,128]{2,1,0:T(8,128)(2,1)S(1)}, bf16[2,128,128]{2,1,0:T(8,128)(2,1)S(1)}, u32[]{:S(2)}, u32[]{:S(2)}) collective-permute-start(bf16[2,128,128]{2,1,0:T(8,128)(2,1)S(1)} %bitcast.61), channel_id=1, source_target_pairs={{0,30},{1,31},{2,0},{3,1},{4,2},{5,3},{6,4},{7,5},{8,6},{9,7},{10,... | collective-permute-start | bytes 196616 | tf_op jit(solution)/shard_map/ppermute | solution.py:16
  20.1 113.1 %all-gather.7.cloned.1.call-start = ((), (), s32[]{:S(2)}) async-start(), calls=%async_computation.1 | async-start | bytes 1081344 | tf_op jit(solution)/shard_map/all_gather | solution.py:52
  42.6 8.5 %copy-start.3 = (s32[112]{0:T(128)S(1)}, s32[112]{0:T(128)}, u32[]{:S(2)}) copy-start(s32[112]{0:T(128)} %param.18) | copy-start | bytes 1348
  72.6 5.9 %copy-start.4 = (s32[32]{0:T(128)S(1)}, s32[32]{0:T(128)}, u32[]{:S(2)}) copy-start(s32[32]{0:T(128)} %param.15) | copy-start | bytes 388
  76.0 3.3 %copy-start.2 = (f32[128,128]{1,0:T(8,128)S(1)}, f32[128,128]{1,0:T(8,128)}, u32[]{:S(2)}) copy-start(f32[128,128]{1,0:T(8,128)} %param.12) | copy-start | bytes 196612
  80.2 8.0 %collective-permute-start.4 = (bf16[2,128,128]{2,1,0:T(8,128)(2,1)S(1)}, bf16[2,128,128]{2,1,0:T(8,128)(2,1)S(1)}, u32[]{:S(2)}, u32[]{:S(2)}) collective-permute-start(bf16[2,128,128]{2,1,0:T(8,128)(2,1)S(1)} %bitcast.65), channel_id=1, source_target_pairs={{0,2},{1,3},{2,4},{3,5},{4,6},{5,7},{6,8},{7,9},{8,10},{9,11},{10,... | collective-permute-start | bytes 196616 | tf_op jit(solution)/shard_map/ppermute | solution.py:16
  81.5 7.4 %collective-permute-start.5 = (bf16[2,128,128]{2,1,0:T(8,128)(2,1)S(1)}, bf16[2,128,128]{2,1,0:T(8,128)(2,1)S(1)}, u32[]{:S(2)}, u32[]{:S(2)}) collective-permute-start(bf16[2,128,128]{2,1,0:T(8,128)(2,1)S(1)} %bitcast.66), channel_id=1, source_target_pairs={{0,1},{1,2},{2,3},{3,4},{4,5},{5,6},{6,7},{7,8},{8,9},{9,10},{10,1... | collective-permute-start | bytes 196616 | tf_op jit(solution)/shard_map/ppermute | solution.py:16
  81.5 7.5 %collective-permute-start.6 = (bf16[2,128,128]{2,1,0:T(8,128)(2,1)S(1)}, bf16[2,128,128]{2,1,0:T(8,128)(2,1)S(1)}, u32[]{:S(2)}, u32[]{:S(2)}) collective-permute-start(bf16[2,128,128]{2,1,0:T(8,128)(2,1)S(1)} %bitcast.67), channel_id=1, source_target_pairs={{0,31},{1,0},{2,1},{3,2},{4,3},{5,4},{6,5},{7,6},{8,7},{9,8},{10,9... | collective-permute-start | bytes 196616 | tf_op jit(solution)/shard_map/ppermute | solution.py:16
  86.9 4.5 %collective-permute-start.7 = (bf16[2,128,128]{2,1,0:T(8,128)(2,1)S(1)}, bf16[2,128,128]{2,1,0:T(8,128)(2,1)S(1)}, u32[]{:S(2)}, u32[]{:S(2)}) collective-permute-start(bf16[2,128,128]{2,1,0:T(8,128)(2,1)S(1)} %bitcast.68), channel_id=1, source_target_pairs={{0,30},{1,31},{2,0},{3,1},{4,2},{5,3},{6,4},{7,5},{8,6},{9,7},{10,... | collective-permute-start | bytes 196616 | tf_op jit(solution)/shard_map/ppermute | solution.py:16
  136.7 3.3 %copy-start.1 = (f32[128,128]{1,0:T(8,128)S(1)}, f32[128,128]{1,0:T(8,128)}, u32[]{:S(2)}) copy-start(f32[128,128]{1,0:T(8,128)} %param.13) | copy-start | bytes 196612
Sparse Core Ops, SparseCore 0:
  20.2 52.2 all-gather.4
  80.3 52.8 all-gather.6
where the time goes:
time: 148 us
  matrix products  38.7 us (26%)
  waiting for transfers between devices  35.3 us (24%)
  local copies, waits for them, and re-layouts  31.9 us (22%)
  between operations  23.9 us (16%)
  starting transfers between devices  16.2 us (11%)
  other arithmetic  1.67 us (1%)
    all_gather x2, waiting for transfers between devices, propagate(): stripe = lax.all_gather(hub_rows, 'blk', axis=0, tiled=True)  31.6 us
    dot_general x4, matrix products, accumulate(): jnp.einsum('sij,sjf->sif', tile_set, inputs, preferred_element_type=jnp.f...  24.5 us
    dot_general x4, local copies, waits for them, and re-layouts, accumulate(): jnp.einsum('sij,sjf->sif', tile_set, inputs, preferred_element_type=jnp.f...  21.8 us
    ppermute x8, starting transfers between devices, from_behind(): lax.ppermute(shard, axis, [(i, (i + by) % size) for i in range(size)])  16.2 us
    dot_general x4, matrix products, accumulate(): jnp.einsum('sn,sif->nif', onehot, products, precision=lax.Precision.HIGHEST)  13 us
    gather x2, local copies, waits for them, and re-layouts, propagate(): gathered_blocks[sparse_src]  5.97 us
    ppermute x8, waiting for transfers between devices, from_behind(): lax.ppermute(shard, axis, [(i, (i + by) % size) for i in range(size)])  3.68 us
  transfers between devices with their start and end apart: 10, of which 6 were waited for; matrix products, arithmetic and copies ran while one was open for 38% of the time, Pallas kernels for 0%

commit v1 on v0

v1 whole, which is shorter than its diff:
```python
import functools
import math

import jax
import jax.numpy as jnp
from jax import lax
from jax.experimental import pallas as pl
from jax.experimental.pallas import tpu as pltpu
from jax.sharding import PartitionSpec as P

F = 128
TILE = 128
HOPS = 2
OFFSETS = list(range(-HOPS, 0)) + list(range(1, HOPS + 1))
MESH = pl.DeviceIdType.MESH
BF16 = jnp.bfloat16
F32 = jnp.float32


def plane_side(chips):
    side = 1
    while chips % ((2 * side) ** 2) == 0 and 2 * (2 * side) ** 3 <= chips:
        side *= 2
    return side


def kernel(
    size, slots,
    dense_row, hub_block, sparse_row, sparse_src, sparse_count, fetch_list,
    features, weight_one, weight_two, dense_hbm, sparse_hbm,
    out,
    feat, weights, dense, sparse, own, spare, stripe, fetched, table, acc,
    load_sem, send_sem, recv_sem, near_send, near_recv,
):
    side = plane_side(size // 2)
    long = size // (2 * side * side)
    me = lax.axis_index("blk")
    core = me % 2
    x = (me // 2) % side
    y = (me // (2 * side)) % side
    z = me // (2 * side * side)
    z_stride = 2 * side * side
    a = x + core * (y - x)
    b = y + core * (x - y)
    a_stride = 2 + core * (2 * side - 2)
    b_stride = 2 * side + core * (2 - 2 * side)

    def at(da, db, dz, other=0):
        return (
            me
            + ((a + da) % side - a) * a_stride
            + ((b + db) % side - b) * b_stride
            + ((z + dz) % long - z) * z_stride
            + other * (1 - 2 * core)
        )

    z_peers = [at(0, 0, k) for k in range(1, long)]
    a_peers = [at(k, 0, 0) for k in range(1, side)]
    b_peers = [at(0, k, 0) for k in range(1, side)]
    twin = at(0, 0, 0, 1)
    owners = [(me + offset + size) % size for offset in OFFSETS]
    readers = [(me - offset + size) % size for offset in OFFSETS]

    barrier = pltpu.get_barrier_semaphore()
    partners = z_peers + a_peers + b_peers + [twin] + owners
    for peer in partners:
        pl.semaphore_signal(barrier, inc=1, device_id=(peer,), device_id_type=MESH)

    loads = [
        pltpu.make_async_copy(features, feat, load_sem.at[0]),
        pltpu.make_async_copy(dense_hbm, dense, load_sem.at[1]),
        pltpu.make_async_copy(sparse_hbm, sparse, load_sem.at[2]),
        pltpu.make_async_copy(weight_one, weights.at[0], load_sem.at[3]),
        pltpu.make_async_copy(weight_two, weights.at[1], load_sem.at[4]),
    ]
    for load in loads:
        load.start()

    table[...] = jnp.zeros_like(table)
    hub_here = hub_block[me]
    live = sparse_count[0]
    dead_key = table.shape[0] - 1
    group = math.gcd(slots, 8)

    loads[0].wait()
    for layer in range(2):
        if layer == 0:
            rows = feat[...].astype(BF16)
        first, second = rows[:TILE], rows[TILE:]
        stripe[layer, me] = jnp.where(hub_here == 0, first, second)
        spare[layer] = jnp.where(hub_here == 0, second, first)
        own[0] = first
        own[1] = second
        if layer == 0:
            pl.semaphore_wait(barrier, len(partners))

        def copy(block, peer):
            return pltpu.make_async_remote_copy(
                src_ref=stripe.at[layer, block],
                dst_ref=stripe.at[layer, block],
                send_sem=send_sem.at[layer],
                recv_sem=recv_sem.at[layer, block],
                device_id=(peer,),
                device_id_type=MESH,
            )

        def near(entry):
            return pltpu.make_async_remote_copy(
                src_ref=spare.at[layer],
                dst_ref=fetched.at[layer, entry],
                send_sem=near_send.at[layer, entry],
                recv_sem=near_recv.at[layer, entry],
                device_id=(readers[entry],),
                device_id_type=MESH,
            )

        def arrive(block):
            copy(block, twin).wait_recv()

        def dense_group(da, db, other):
            blocks = [at(da, db, dz, other) for dz in range(long)]
            left = jnp.concatenate([dense[block] for block in blocks], axis=1)
            right = []
            for block in blocks:
                held = stripe[layer, block]
                row = dense_row[block]
                blank = jnp.zeros_like(held)
                right.append(
                    jnp.concatenate(
                        [jnp.where(row == 0, held, blank), jnp.where(row == 1, held, blank)], axis=1
                    )
                )
            acc[...] += jnp.dot(left, jnp.concatenate(right, axis=0), preferred_element_type=F32)

        for peer in a_peers + b_peers + z_peers + [twin]:
            copy(me, peer).start()
        for entry in range(len(OFFSETS)):
            near(entry).start()
        for source in (0, 1):
            for row in (0, 1):
                table[2 * source + row, :, row * F : (row + 1) * F] = own[source]
        acc[...] = jnp.zeros_like(acc)

        def from_a(da, dz):
            block = at(da, 0, dz)
            arrive(block)
            for peer in b_peers + [twin]:
                copy(block, peer).start()

        for da in range(1, side):
            from_a(da, 0)

        @pl.loop(1, long)
        def _(dz):
            block = at(0, 0, dz)
            arrive(block)
            for peer in a_peers + b_peers + [twin]:
                copy(block, peer).start()

        for da in range(1, side):

            @pl.loop(1, long)
            def _(dz):
                from_a(da, dz)

        if layer == 0:
            loads[1].wait()
        dense_group(0, 0, 0)
        for db in range(1, side):
            for da in range(side):

                @pl.loop(0, long)
                def _(dz):
                    block = at(da, db, dz)
                    arrive(block)
                    copy(block, twin).start()

        for da in range(1, side):
            dense_group(da, 0, 0)
        for db in range(1, side):
            for da in range(side):
                dense_group(da, db, 0)

        for db in range(side):
            for da in range(side):

                @pl.loop(0, long)
                def _(dz):
                    arrive(at(da, db, dz, 1))

                dense_group(da, db, 1)

        for entry in range(len(OFFSETS)):
            near(entry).wait_recv()
            owner = owners[entry]
            block = jnp.where(
                fetch_list[0, entry] == hub_block[owner], stripe[layer, owner], fetched[layer, entry]
            )
            for row in (0, 1):
                table[2 * (entry + 2) + row, :, row * F : (row + 1) * F] = block
        if layer == 0:
            loads[2].wait()

        @pl.loop(0, slots // group)
        def _(step):
            left, right = [], []
            for inner in range(group):
                slot = step * group + inner
                key = jnp.where(slot < live, 2 * sparse_src[slot] + sparse_row[slot], dead_key)
                left.append(sparse[slot])
                right.append(table[key])
            acc[...] += jnp.dot(
                jnp.concatenate(left, axis=1),
                jnp.concatenate(right, axis=0),
                preferred_element_type=F32,
            )

        if layer == 0:
            loads[3].wait()
            loads[4].wait()
        summed = jnp.concatenate([acc[:, :F], acc[:, F:]], axis=0)
        weight = weights[layer]
        high = summed.astype(BF16)
        low = (summed - high.astype(F32)).astype(BF16)
        weight_high = weight.astype(BF16)
        weight_low = (weight - weight_high.astype(F32)).astype(BF16)
        projected = jnp.dot(
            jnp.concatenate([high, low, high], axis=1),
            jnp.concatenate([weight_high, weight_high, weight_low], axis=0),
            preferred_element_type=F32,
        )
        result = jnp.maximum(projected, 0.0)
        if layer == 0:
            rows = result.astype(BF16)
        else:
            out[...] = result

    for layer in range(2):
        sent = stripe.at[layer, pl.ds(0, size - 1)]
        pltpu.make_async_copy(sent, sent, send_sem.at[layer]).wait()
        for entry in range(len(OFFSETS)):
            pltpu.make_async_remote_copy(
                src_ref=spare.at[layer],
                dst_ref=fetched.at[layer, entry],
                send_sem=near_send.at[layer, entry],
                recv_sem=near_recv.at[layer, entry],
                device_id=(readers[entry],),
                device_id_type=MESH,
            ).wait_send()


def shards(
    size, features, weight_one, weight_two, dense_tiles, dense_row, hub_block,
    sparse_tiles, sparse_row, sparse_src, sparse_count, fetch_list,
):
    slots = sparse_tiles.shape[0]
    nodes = features.shape[0]
    near = len(OFFSETS)
    smem = pl.BlockSpec(memory_space=pltpu.SMEM)
    hbm = pl.BlockSpec(memory_space=pl.ANY)
    return pl.pallas_call(
        functools.partial(kernel, size, slots),
        out_shape=jax.ShapeDtypeStruct((nodes, F), F32),
        in_specs=[smem] * 6 + [hbm] * 5,
        out_specs=pl.BlockSpec(memory_space=pltpu.VMEM),
        scratch_shapes=[
            pltpu.VMEM((nodes, F), F32),
            pltpu.VMEM((2, F, F), F32),
            pltpu.VMEM(dense_tiles.shape, BF16),
            pltpu.VMEM(sparse_tiles.shape, BF16),
            pltpu.VMEM((2, TILE, F), BF16),
            pltpu.VMEM((2, TILE, F), BF16),
            pltpu.VMEM((2, size, TILE, F), BF16),
            pltpu.VMEM((2, near, TILE, F), BF16),
            pltpu.VMEM((2 * (2 + near) + 1, TILE, 2 * F), BF16),
            pltpu.VMEM((TILE, 2 * F), F32),
            pltpu.SemaphoreType.DMA((5,)),
            pltpu.SemaphoreType.DMA((2,)),
            pltpu.SemaphoreType.DMA((2, size)),
            pltpu.SemaphoreType.DMA((2, near)),
            pltpu.SemaphoreType.DMA((2, near)),
        ],
        compiler_params=pltpu.CompilerParams(
            collective_id=0, has_side_effects=True, vmem_limit_bytes=56 * 2**20
        ),
    )(
        dense_row, hub_block, sparse_row, sparse_src, sparse_count, fetch_list,
        features, weight_one, weight_two, dense_tiles, sparse_tiles,
    )


def solution(mesh):
    size = mesh.shape["blk"]
    placed = (
        P("blk", None),
        P(),
        P(),
        P("blk", None, None),
        P("blk"),
        P(),
        P("blk", None, None),
        P("blk"),
        P("blk"),
        P("blk"),
        P("blk", None),
    )
    return jax.shard_map(
        functools.partial(shards, size),
        mesh=mesh, in_specs=placed, out_specs=P("blk", None), check_vma=False,
    )
```

time: 148 us -> 43.3 us (0.29)
  Pallas kernels: 0 us -> 40.9 us
  matrix products: 38.7 us -> 0 us
  waiting for transfers between devices: 35.3 us -> 0 us
  local copies, waits for them, and re-layouts: 31.9 us -> 1.57 us
  between operations: 23.9 us -> 0.66 us
  starting transfers between devices: 16.2 us -> 0 us
  other arithmetic: 1.67 us -> 0 us
    pallas_call x0 -> x1, Pallas kernels: none -> 40.9 us  [shards(): pl.pallas_call(functools.partial(kernel, size, slots), out_shape=jax.Shap...]
    dot_general x10 -> x0, matrix products: 38.7 us -> none  [the longest x4 24.5 us: accumulate(): jnp.einsum('sij,sjf->sif', tile_set, inputs, preferred_element_type=jnp.f...]
    all_gather x2 -> x0, waiting for transfers between devices: 31.6 us -> none  [propagate(): stripe = lax.all_gather(hub_rows, 'blk', axis=0, tiled=True)]
    dot_general x4 -> x0, local copies, waits for them, and re-layouts: 21.8 us -> none  [accumulate(): jnp.einsum('sij,sjf->sif', tile_set, inputs, preferred_element_type=jnp.f...]
    ppermute x8 -> x0, starting transfers between devices: 16.2 us -> none  [from_behind(): lax.ppermute(shard, axis, [(i, (i + by) % size) for i in range(size)])]
    gather x2 -> x0, local copies, waits for them, and re-layouts: 5.97 us -> none  [propagate(): gathered_blocks[sparse_src]]
    ppermute x8 -> x0, waiting for transfers between devices: 3.68 us -> none  [from_behind(): lax.ppermute(shard, axis, [(i, (i + by) % size) for i in range(size)])]
    dynamic_slice x3 -> x0, local copies, waits for them, and re-layouts: 2.48 us -> none  [the longest x2 1.25 us: propagate(): hub_rows = lax.dynamic_index_in_dim(blocks, hub_here, 0, keepdims=False)]
  transfers between devices with their start and end apart: 10 -> 0, of which waited for: 6 -> 0; matrix products, arithmetic and copies ran while one was open for 38% -> 0% of each run, Pallas kernels for 0% -> 0%
where the time goes in v1:
time: 43.3 us; the launch traced here: 43.2 us
  Pallas kernels  40.9 us (94%)
  local copies, waits for them, and re-layouts  1.57 us (4%)
  between operations  0.66 us (2%)
    pallas_call x1, Pallas kernels, shards(): pl.pallas_call(functools.partial(kernel, size, slots), out_shape=jax.Shap...  40.9 us
    unnamed x1, local copies, waits for them, and re-layouts  1.57 us

profile of v1, /device:TPU:0, one launch (start us, length us, event | category | flops | bytes accessed | tf_op | source)
XLA Modules:
  0.0 43.2 jit_solution(17465176193644692411)
XLA Ops:
  0.7 40.9 %shard_map.109 = f32[256,128]{1,0:T(8,128)} custom-call(s32[32]{0:T(128)} %dense_row.1, s32[32]{0:T(128)} %hub_block.1, s32[112]{0:T(128)} %sparse_row.1, s32[112]{0:T(128)} %sparse_src.1, s32[1]{0:T(128)S(6)} %copy.13.sparse_count, s32[1,4]{1,0:T(1,128)} %fetch_list.1, f32[256,128]{1,0:T(8,128)} %features.1, f32[128,128]{1,0:T(8,128)} %weight_one.1, ...), custom_call_target="tpu_custom_call" | custom-call | tf_op jit(solution)/shard_map/pallas_call | solution.py:261
  41.6 1.6 %copy.14 = f32[256,128]{1,0:T(8,128)} copy(f32[256,128]{1,0:T(8,128)} %shard_map.109) | data formatting | bytes 262144

commit v2 on v1

v2 whole, which is shorter than its diff:
```python
import functools
import math

import jax
import jax.numpy as jnp
from jax import lax
from jax.experimental import pallas as pl
from jax.experimental.pallas import tpu as pltpu
from jax.sharding import PartitionSpec as P

F = 128
TILE = 128
HOPS = 2
OFFSETS = list(range(-HOPS, 0)) + list(range(1, HOPS + 1))
MESH = pl.DeviceIdType.MESH
DIRECT = ()
BF16 = jnp.bfloat16
F32 = jnp.float32


def plane_side(chips):
    side = 1
    while chips % ((2 * side) ** 2) == 0 and 2 * (2 * side) ** 3 <= chips:
        side *= 2
    return side


def kernel(
    size, slots,
    dense_row, hub_block, sparse_count, fetch_list, sparse_row, sparse_src,
    features, weight_one, weight_two, dense_hbm, sparse_hbm,
    out,
    feat, weights, dense, sparse, spare, stripe, fetched, sums, adjacency, near_blocks,
    acc, lists, order, load_sem, send_sem, recv_sem, near_send, near_recv,
):
    side = plane_side(size // 2)
    long = size // (2 * side * side)
    me = lax.axis_index("blk")
    core = me % 2
    x = (me // 2) % side
    y = (me // (2 * side)) % side
    z = me // (2 * side * side)
    z_stride = 2 * side * side
    def at(dx, dy, dz, other=0):
        return (
            me
            + ((x + dx) % side - x) * 2
            + ((y + dy) % side - y) * 2 * side
            + ((z + dz) % long - z) * z_stride
            + other * (1 - 2 * core)
        )

    plane = [(dx, dy) for dy in range(side) for dx in range(side)][1:]
    direct = [dz for dz in DIRECT if dz < long]
    relayed = [dz for dz in range(1, long) if dz not in direct]
    twin = at(0, 0, 0, 1)
    owners = [(me + offset + size) % size for offset in OFFSETS]
    readers = [(me - offset + size) % size for offset in OFFSETS]

    barrier = pltpu.get_barrier_semaphore()
    partners = [at(0, 0, dz) for dz in range(1, long)] + [twin] + owners
    partners += [at(dx, dy, 0) for dx, dy in plane]
    for dz in direct:
        partners += [at(dx, dy, dz) for dx, dy in plane]
        partners += [at(dx, dy, -dz) for dx, dy in plane]
    for peer in partners:
        pl.semaphore_signal(barrier, inc=1, device_id=(peer,), device_id_type=MESH)

    loads = [
        pltpu.make_async_copy(features, feat, load_sem.at[0]),
        pltpu.make_async_copy(dense_hbm, dense, load_sem.at[1]),
        pltpu.make_async_copy(sparse_hbm, sparse, load_sem.at[2]),
        pltpu.make_async_copy(weight_one, weights.at[0], load_sem.at[3]),
        pltpu.make_async_copy(weight_two, weights.at[1], load_sem.at[4]),
    ]
    for load in loads:
        load.start()

    hub_here = hub_block[me]

    pairs = 2 * (2 + len(OFFSETS))
    row_wise = lax.broadcasted_iota(jnp.int32, (slots, slots), 0)
    lane_wise = lax.broadcasted_iota(jnp.int32, (slots, slots), 1)
    places = lax.broadcasted_iota(jnp.int32, (1, slots), 1)
    keys = jnp.where(places < sparse_count[0], 2 * sparse_src[...] + sparse_row[...], pairs)
    keys = jnp.broadcast_to(keys, (slots, slots))
    key_of_row = jnp.sum(jnp.where(row_wise == lane_wise, keys, 0), axis=1, keepdims=True)
    ahead = (keys < key_of_row) | ((keys == key_of_row) & (lane_wise < row_wise))
    rank = jnp.sum(jnp.where(ahead, 1, 0), axis=1, keepdims=True)
    lists[0:1, 0:slots] = jnp.sum(jnp.where(rank == lane_wise, row_wise, 0), axis=0, keepdims=True)
    lists[1:2, 0:slots] = jnp.sum(jnp.where(key_of_row < lane_wise, 1, 0), axis=0, keepdims=True)
    to_scalars = pltpu.make_async_copy(lists, order, load_sem.at[5])
    to_scalars.start()
    group = math.gcd(slots, 8)

    loads[0].wait()
    for layer in range(2):
        if layer == 0:
            rows = feat[...].astype(BF16)
        first, second = rows[:TILE], rows[TILE:]
        stripe[layer, me] = jnp.where(hub_here == 0, first, second)
        spare[layer] = jnp.where(hub_here == 0, second, first)
        near_blocks[0:TILE] = first
        near_blocks[TILE : 2 * TILE] = second
        if layer == 0:
            pl.semaphore_wait(barrier, len(partners))

        def copy(block, peer):
            return pltpu.make_async_remote_copy(
                src_ref=stripe.at[layer, block],
                dst_ref=stripe.at[layer, block],
                send_sem=send_sem.at[layer],
                recv_sem=recv_sem.at[layer, block],
                device_id=(peer,),
                device_id_type=MESH,
            )

        def near(entry):
            return pltpu.make_async_remote_copy(
                src_ref=spare.at[layer],
                dst_ref=fetched.at[layer, entry],
                send_sem=near_send.at[layer, entry],
                recv_sem=near_recv.at[layer, entry],
                device_id=(readers[entry],),
                device_id_type=MESH,
            )

        def arrive(block):
            copy(block, twin).wait_recv()

        def dense_group(dx, dy, other):
            blocks = [at(dx, dy, dz, other) for dz in range(long)]
            left = jnp.concatenate([dense[block] for block in blocks], axis=1)
            right = []
            for block in blocks:
                held = stripe[layer, block]
                row = dense_row[block]
                blank = jnp.zeros_like(held)
                right.append(
                    jnp.concatenate(
                        [jnp.where(row == 0, held, blank), jnp.where(row == 1, held, blank)], axis=1
                    )
                )
            acc[...] += jnp.dot(left, jnp.concatenate(right, axis=0), preferred_element_type=F32)

        for dz in relayed:
            copy(me, at(0, 0, dz)).start()
        for dx, dy in plane:
            copy(me, at(dx, dy, 0)).start()
        for dz in direct:
            for dx, dy in [(0, 0)] + plane:
                copy(me, at(dx, dy, dz)).start()
        copy(me, twin).start()
        for entry in range(len(OFFSETS)):
            near(entry).start()
        acc[...] = jnp.zeros_like(acc)

        for dz in relayed:
            block = at(0, 0, -dz)
            arrive(block)
            for dx, dy in plane:
                copy(block, at(dx, dy, 0)).start()
            copy(block, twin).start()
        for dx, dy in plane:
            block = at(dx, dy, 0)
            arrive(block)
            copy(block, twin).start()
        for dz in direct:
            for dx, dy in [(0, 0)] + plane:
                block = at(dx, dy, -dz)
                arrive(block)
                copy(block, twin).start()

        if layer == 0:
            loads[1].wait()
            loads[2].wait()
            to_scalars.wait()
            sums[0] = jnp.zeros((TILE, TILE), F32)

            @pl.loop(0, slots // group)
            def _(step):
                running = sums[step * group]
                for inner in range(group):
                    place = step * group + inner
                    running = running + sparse[order[0, place]].astype(F32)
                    sums[place + 1] = running

            for pair in range(pairs):
                source, row = pair // 2, pair % 2
                total = sums[order[1, pair + 1]] - sums[order[1, pair]]
                high = total.astype(BF16)
                low = (total - high.astype(F32)).astype(BF16)
                here = pl.ds(row * TILE, TILE)
                adjacency[0, here, source * TILE : (source + 1) * TILE] = high
                adjacency[1, here, source * TILE : (source + 1) * TILE] = low
        dense_group(0, 0, 0)

        for dx, dy in plane:
            for dz in relayed:
                block = at(dx, dy, -dz)
                arrive(block)
                copy(block, twin).start()
        for dx, dy in plane:
            dense_group(dx, dy, 0)

        for dx, dy in [(0, 0)] + plane:
            for dz in range(long):
                arrive(at(dx, dy, dz, 1))
            dense_group(dx, dy, 1)

        for entry in range(len(OFFSETS)):
            near(entry).wait_recv()
            owner = owners[entry]
            near_blocks[(entry + 2) * TILE : (entry + 3) * TILE] = jnp.where(
                fetch_list[0, entry] == hub_block[owner], stripe[layer, owner], fetched[layer, entry]
            )
        blocks = near_blocks[...]
        summed = jnp.concatenate([acc[:, :F], acc[:, F:]], axis=0)
        summed += jnp.dot(adjacency[0], blocks, preferred_element_type=F32)
        summed += jnp.dot(adjacency[1], blocks, preferred_element_type=F32)

        if layer == 0:
            loads[3].wait()
            loads[4].wait()
        weight = weights[layer]
        high = summed.astype(BF16)
        low = (summed - high.astype(F32)).astype(BF16)
        weight_high = weight.astype(BF16)
        weight_low = (weight - weight_high.astype(F32)).astype(BF16)
        projected = jnp.dot(
            jnp.concatenate([high, low, high], axis=1),
            jnp.concatenate([weight_high, weight_high, weight_low], axis=0),
            preferred_element_type=F32,
        )
        result = jnp.maximum(projected, 0.0)
        if layer == 0:
            rows = result.astype(BF16)
        else:
            out[...] = result

    for layer in range(2):
        sent = stripe.at[layer, pl.ds(0, size - 1)]
        pltpu.make_async_copy(sent, sent, send_sem.at[layer]).wait()
        for entry in range(len(OFFSETS)):
            pltpu.make_async_remote_copy(
                src_ref=spare.at[layer],
                dst_ref=fetched.at[layer, entry],
                send_sem=near_send.at[layer, entry],
                recv_sem=near_recv.at[layer, entry],
                device_id=(readers[entry],),
                device_id_type=MESH,
            ).wait_send()


def shards(
    size, features, weight_one, weight_two, dense_tiles, dense_row, hub_block,
    sparse_tiles, sparse_row, sparse_src, sparse_count, fetch_list,
):
    slots = sparse_tiles.shape[0]
    nodes = features.shape[0]
    near = len(OFFSETS)
    smem = pl.BlockSpec(memory_space=pltpu.SMEM)
    vmem = pl.BlockSpec(memory_space=pltpu.VMEM)
    hbm = pl.BlockSpec(memory_space=pl.ANY)
    return pl.pallas_call(
        functools.partial(kernel, size, slots),
        out_shape=jax.ShapeDtypeStruct((nodes, F), F32),
        in_specs=[smem] * 4 + [vmem] * 2 + [hbm] * 5,
        out_specs=vmem,
        scratch_shapes=[
            pltpu.VMEM((nodes, F), F32),
            pltpu.VMEM((2, F, F), F32),
            pltpu.VMEM(dense_tiles.shape, BF16),
            pltpu.VMEM(sparse_tiles.shape, BF16),
            pltpu.VMEM((2, TILE, F), BF16),
            pltpu.VMEM((2, size, TILE, F), BF16),
            pltpu.VMEM((2, near, TILE, F), BF16),
            pltpu.VMEM((slots + 1, TILE, TILE), F32),
            pltpu.VMEM((2, 2 * TILE, (2 + near) * TILE), BF16),
            pltpu.VMEM(((2 + near) * TILE, F), BF16),
            pltpu.VMEM((TILE, 2 * F), F32),
            pltpu.VMEM((8, 128), jnp.int32),
            pltpu.SMEM((8, 128), jnp.int32),
            pltpu.SemaphoreType.DMA((6,)),
            pltpu.SemaphoreType.DMA((2,)),
            pltpu.SemaphoreType.DMA((2, size)),
            pltpu.SemaphoreType.DMA((2, near)),
            pltpu.SemaphoreType.DMA((2, near)),
        ],
        compiler_params=pltpu.CompilerParams(
            collective_id=0, has_side_effects=True, vmem_limit_bytes=56 * 2**20
        ),
    )(
        dense_row, hub_block, sparse_count, fetch_list,
        sparse_row.reshape(1, slots), sparse_src.reshape(1, slots),
        features, weight_one, weight_two, dense_tiles, sparse_tiles,
    )


def solution(mesh):
    size = mesh.shape["blk"]
    placed = (
        P("blk", None),
        P(),
        P(),
        P("blk", None, None),
        P("blk"),
        P(),
        P("blk", None, None),
        P("blk"),
        P("blk"),
        P("blk"),
        P("blk", None),
    )
    return jax.shard_map(
        functools.partial(shards, size),
        mesh=mesh, in_specs=placed, out_specs=P("blk", None), check_vma=False,
    )
```

time: 43.3 us -> 35.1 us (0.81)
  Pallas kernels: 40.9 us -> 32.6 us
    pallas_call x1, Pallas kernels: 40.9 us -> 32.6 us  [shards(): pl.pallas_call(functools.partial(kernel, size, slots), out_shape=jax.Shap...]
where the time goes in v2:
time: 35.1 us; the launch traced here: 34.8 us
  Pallas kernels  32.6 us (93%)
  local copies, waits for them, and re-layouts  1.57 us (4%)
  between operations  0.66 us (2%)
    pallas_call x1, Pallas kernels, shards(): pl.pallas_call(functools.partial(kernel, size, slots), out_shape=jax.Shap...  32.6 us
    unnamed x1, local copies, waits for them, and re-layouts  1.57 us

profile of v2, /device:TPU:0, one launch (start us, length us, event | category | flops | bytes accessed | tf_op | source)
XLA Modules:
  0.0 34.8 jit_solution(10352786963221795787)
XLA Ops:
  0.7 32.6 %shard_map.109 = f32[256,128]{1,0:T(8,128)} custom-call(s32[32]{0:T(128)} %dense_row.1, s32[32]{0:T(128)} %hub_block.1, s32[1]{0:T(128)S(6)} %copy.13.sparse_count, s32[1,4]{1,0:T(1,128)} %fetch_list.1, s32[1,112]{1,0:T(1,128)} %bitcast.2, s32[1,112]{1,0:T(1,128)} %bitcast.3, f32[256,128]{1,0:T(8,128)} %features.1, f32[128,128]{1,0:T(8,128)} %weight_one.1, ...), custom_call_target="tpu_custom_call" | custom-call | tf_op jit(solution)/shard_map/pallas_call | solution.py:265
  33.2 1.6 %copy.14 = f32[256,128]{1,0:T(8,128)} copy(f32[256,128]{1,0:T(8,128)} %shard_map.109) | data formatting | bytes 262144

commit v3 on v2

--- a/solution.py
+++ b/solution.py
@@ -55,10 +55,12 @@
     relayed = [dz for dz in range(1, long) if dz not in direct]
     twin = at(0, 0, 0, 1)
     owners = [(me + offset + size) % size for offset in OFFSETS]
-    readers = [(me - offset + size) % size for offset in OFFSETS]
+    far = [0, len(OFFSETS) - 1]
+    relay_entry = 3 * (1 - core)
 
     barrier = pltpu.get_barrier_semaphore()
-    partners = [at(0, 0, dz) for dz in range(1, long)] + [twin] + owners
+    partners = [at(0, 0, dz) for dz in range(1, long)] + [twin]
+    partners += [owners[entry] for entry in far]
     partners += [at(dx, dy, 0) for dx, dy in plane]
     for dz in direct:
         partners += [at(dx, dy, dz) for dx, dy in plane]
@@ -115,15 +117,18 @@
                 device_id_type=MESH,
             )
 
-        def near(entry):
+        def near(source, entry, peer, sem):
             return pltpu.make_async_remote_copy(
-                src_ref=spare.at[layer],
+                src_ref=source,
                 dst_ref=fetched.at[layer, entry],
-                send_sem=near_send.at[layer, entry],
+                send_sem=near_send.at[layer, sem],
                 recv_sem=near_recv.at[layer, entry],
-                device_id=(readers[entry],),
+                device_id=(peer,),
                 device_id_type=MESH,
             )
+
+        def near_arrive(entry):
+            near(spare.at[layer], entry, twin, 0).wait_recv()
 
         def arrive(block):
             copy(block, twin).wait_recv()
@@ -151,8 +156,9 @@
             for dx, dy in [(0, 0)] + plane:
                 copy(me, at(dx, dy, dz)).start()
         copy(me, twin).start()
-        for entry in range(len(OFFSETS)):
-            near(entry).start()
+        near(spare.at[layer], 0, owners[3], 0).start()
+        near(spare.at[layer], 3, owners[0], 1).start()
+        near(spare.at[layer], 1 + core, twin, 2).start()
         acc[...] = jnp.zeros_like(acc)
 
         for dz in relayed:
@@ -171,6 +177,9 @@
                 arrive(block)
                 copy(block, twin).start()
 
+        near_arrive(relay_entry)
+        near(fetched.at[layer, relay_entry], 2 - core, twin, 3).start()
+
         if layer == 0:
             loads[1].wait()
             loads[2].wait()
@@ -208,8 +217,10 @@
                 arrive(at(dx, dy, dz, 1))
             dense_group(dx, dy, 1)
 
+        near_arrive(3 - relay_entry)
+        near_arrive(1)
+        near_arrive(2)
         for entry in range(len(OFFSETS)):
-            near(entry).wait_recv()
             owner = owners[entry]
             near_blocks[(entry + 2) * TILE : (entry + 3) * TILE] = jnp.where(
                 fetch_list[0, entry] == hub_block[owner], stripe[layer, owner], fetched[layer, entry]
@@ -232,11 +243,10 @@
             jnp.concatenate([weight_high, weight_high, weight_low], axis=0),
             preferred_element_type=F32,
         )
-        result = jnp.maximum(projected, 0.0)
-        if layer == 0:
-            rows = result.astype(BF16)
+        if layer == 0:
+            rows = jnp.maximum(projected, 0.0).astype(BF16)
         else:
-            out[...] = result
+            out[...] = projected
 
     for layer in range(2):
         sent = stripe.at[layer, pl.ds(0, size - 1)]
@@ -247,7 +257,7 @@
                 dst_ref=fetched.at[layer, entry],
                 send_sem=near_send.at[layer, entry],
                 recv_sem=near_recv.at[layer, entry],
-                device_id=(readers[entry],),
+                device_id=(twin,),
                 device_id_type=MESH,
             ).wait_send()
 
@@ -262,7 +272,7 @@
     smem = pl.BlockSpec(memory_space=pltpu.SMEM)
     vmem = pl.BlockSpec(memory_space=pltpu.VMEM)
     hbm = pl.BlockSpec(memory_space=pl.ANY)
-    return pl.pallas_call(
+    projected = pl.pallas_call(
         functools.partial(kernel, size, slots),
         out_shape=jax.ShapeDtypeStruct((nodes, F), F32),
         in_specs=[smem] * 4 + [vmem] * 2 + [hbm] * 5,
@@ -295,6 +305,7 @@
         sparse_row.reshape(1, slots), sparse_src.reshape(1, slots),
         features, weight_one, weight_two, dense_tiles, sparse_tiles,
     )
+    return jax.nn.relu(projected)
 
 
 def solution(mesh):

time: 35.1 us -> 34.6 us (0.986)
  other arithmetic: 0 us -> 1.57 us
  local copies, waits for them, and re-layouts: 1.57 us -> 0 us
  Pallas kernels: 32.6 us -> 32.1 us
    max x0 -> x1, other arithmetic: none -> 1.57 us  [shards(): return jax.nn.relu(projected)]
    unnamed x1 -> x0, local copies, waits for them, and re-layouts: 1.57 us -> none
    pallas_call x1, Pallas kernels: 32.6 us -> 32.1 us  [shards(): pl.pallas_call(functools.partial(kernel, size, slots), out_shape=jax.Shap...]
where the time goes in v3:
time: 34.6 us; the launch traced here: 34.3 us
  Pallas kernels  32.1 us (93%)
  other arithmetic  1.57 us (5%)
  between operations  0.66 us (2%)
    pallas_call x1, Pallas kernels, shards(): pl.pallas_call(functools.partial(kernel, size, slots), out_shape=jax.Shap...  32.1 us
    max x1, other arithmetic, shards(): return jax.nn.relu(projected)  1.57 us

profile of v3, /device:TPU:0, one launch (start us, length us, event | category | flops | bytes accessed | tf_op | source)
XLA Modules:
  0.0 34.3 jit_solution(1838638302233328698)
XLA Ops:
  0.7 32.1 %shard_map.109 = f32[256,128]{1,0:T(8,128)} custom-call(s32[32]{0:T(128)} %dense_row.1, s32[32]{0:T(128)} %hub_block.1, s32[1]{0:T(128)S(6)} %copy.12.sparse_count, s32[1,4]{1,0:T(1,128)} %fetch_list.1, s32[1,112]{1,0:T(1,128)} %bitcast.2, s32[1,112]{1,0:T(1,128)} %bitcast.3, f32[256,128]{1,0:T(8,128)} %features.1, f32[128,128]{1,0:T(8,128)} %weight_one.1, ...), custom_call_target="tpu_custom_call" | custom-call | tf_op jit(solution)/shard_map/pallas_call | solution.py:275
  32.8 1.6 %broadcast_maximum_fusion = f32[256,128]{1,0:T(8,128)} fusion(f32[256,128]{1,0:T(8,128)} %shard_map.109), kind=kLoop, calls=%fused_computation | loop fusion | flops 32768 | bytes 262144 | tf_op jit(solution)/shard_map/jit(relu)/max | solution.py:308
